TPU v7x, 256 devices: a whole 4x4x8 slice. The times are simulated.
256 devices in a mesh: section: 32 (over y, z_lo, core), tp: 8 (over z_hi, x).
Axes of the slice: x: 4, y: 4, z: 8 (z_hi: 2, z_lo: 4; z = z_hi * 4 + z_lo), core: 2. Of those that a mesh axis runs over, the one named last changes fastest.
Arguments:
- held_rows: bfloat16 [32, 256, 4096], P('section', 'tp'), may hold values from -17 to 17
- entering: bfloat16 [3, 256, 4096], P(None, 'tp'), may hold values from -17 to 17
- norm_gain: bfloat16 [32, 4096], P('section'), may hold values from 0.099609375 to 1.8984375
- w_query: bfloat16 [32, 4096, 4096], P('section', None, 'tp'), may hold values from -0.09375 to 0.09375
- b_query: bfloat16 [32, 4096], P('section', 'tp'), may hold values from -8 to 8
- w_keyval: bfloat16 [32, 4096, 2048], P('section', None, 'tp'), may hold values from -0.09375 to 0.09375
- b_keyval: bfloat16 [32, 2048], P('section', 'tp'), may hold values from -3 to 3
- w_out: bfloat16 [32, 4096, 4096], P('section', 'tp'), may hold values from -0.09375 to 0.09375
- prefix_keys: bfloat16 [32, 4, 512, 1024], P('section', None, None, 'tp'), may hold values from -8 to 8
- prefix_values: bfloat16 [32, 4, 512, 1024], P('section', None, None, 'tp'), may hold values from -5 to 5
- lengths: int32 [35], replicated, may hold values from 128 to 512, as said below
Outputs:
- leaving: bfloat16 [32, 256, 4096], P('section', 'tp')
- new_cache: bfloat16 [32, 4, 256, 2048], P('section', None, None, 'tp')
Inputs may be any that keep to these rules, and one draw needn't show every extreme that they name: `lengths`: some block sees all 512 cached slots.
All inputs are finite; a program needn't handle non-finite values.
Results may differ from a plain program's by a relative error of at most 0.022.
Values may be sent and summed in bfloat16 or wider, within the bound.
A program may use at most 64 MiB of HBM per device.

v0:
```python
import math

import jax
import jax.numpy as jnp
from jax import lax
from jax.sharding import PartitionSpec as P

HEAD_DIM = 128


rope_base = 1000000.0
norm_eps = 1e-06


def from_behind(value, axis, steps):
    count = lax.axis_size(axis)
    pairs = [(source, (source + steps) % count) for source in range(count)]
    return lax.ppermute(value, axis, pairs)


def normalize(row_block, gain_row):
    widened = row_block.astype(jnp.float32)
    mean_square = jnp.mean(widened * widened, axis=-1, keepdims=True)
    return (widened * lax.rsqrt(mean_square + norm_eps) * gain_row.astype(jnp.float32)).astype(
        jnp.bfloat16
    )


def rotate(vectors, positions):
    half_dim = vectors.shape[-1] // 2
    frequency = jnp.exp(
        -(jnp.arange(half_dim, dtype=jnp.float32) * 2.0 / vectors.shape[-1]) * math.log(rope_base)
    )
    angles = positions[:, None] * frequency[None, :]
    cosine = jnp.cos(angles)[:, None, :]
    sine_part = jnp.sin(angles)[:, None, :]
    first_half = vectors[..., :half_dim]
    second_half = vectors[..., half_dim:]
    return jnp.concatenate(
        [
            first_half * cosine - second_half * sine_part,
            second_half * cosine + first_half * sine_part,
        ],
        axis=-1,
    )


def attend(projected, cached_keys, cached_values, offset, query_heads, key_heads, head_dim):
    row_count = projected.shape[0]
    slot_count = cached_keys.shape[0]
    query_cols = query_heads * head_dim
    queries = projected[:, :query_cols].reshape(row_count, query_heads, head_dim)
    key_value = projected[:, query_cols:].reshape(row_count, key_heads, 2, head_dim)
    positions = (offset + jnp.arange(row_count, dtype=jnp.int32)).astype(jnp.float32)
    turned_query = rotate(queries, positions).astype(jnp.bfloat16)
    turned_keys = rotate(key_value[:, :, 0], positions).astype(jnp.bfloat16)
    value_part = key_value[:, :, 1].astype(jnp.bfloat16)
    block_cache = jnp.stack([turned_keys, value_part], axis=2).reshape(
        row_count, key_heads * 2 * head_dim
    )
    key_rows = jnp.concatenate(
        [cached_keys.reshape(slot_count, key_heads, head_dim), turned_keys], axis=0
    )
    value_rows = jnp.concatenate(
        [cached_values.reshape(slot_count, key_heads, head_dim), value_part], axis=0
    )
    grouped = turned_query.reshape(row_count, key_heads, query_heads // key_heads, head_dim)
    scores = jnp.einsum(
        "qkgd,skd->kgqs", grouped, key_rows, preferred_element_type=jnp.float32
    ) * head_dim ** (-0.5)
    slot_index = jnp.arange(slot_count + row_count, dtype=jnp.int32)
    row_index = jnp.arange(row_count, dtype=jnp.int32)
    allowed = jnp.where(
        slot_index[None, :] < slot_count,
        slot_index[None, :] < offset,
        slot_index[None, :] - slot_count <= row_index[:, None],
    )
    scores = jnp.where(allowed, scores, jnp.float32(-1e30))
    top_score = jnp.max(scores, axis=-1, keepdims=True)
    weights = jnp.exp(scores - top_score)
    softmax_weights = (weights / jnp.sum(weights, axis=-1, keepdims=True)).astype(jnp.bfloat16)
    attended = jnp.einsum(
        "kgqs,skd->qkgd", softmax_weights, value_rows, preferred_element_type=jnp.float32
    )
    return (block_cache, attended.reshape(row_count, query_heads * head_dim).astype(jnp.bfloat16))


def shards(
    held_rows,
    entering,
    norm_gain,
    w_query,
    b_query,
    w_keyval,
    b_keyval,
    w_out,
    prefix_keys,
    prefix_values,
    lengths,
):
    section_count = lax.axis_size("section")
    section_id = lax.axis_index("section")
    member = lax.axis_index("tp")
    shard_count = held_rows.shape[1]
    block_count = prefix_keys.shape[1]
    query_weight = w_query[0]
    query_bias = b_query[0].astype(jnp.float32)
    keyval_weight = w_keyval[0]
    keyval_bias = b_keyval[0].astype(jnp.float32)
    out_weight = w_out[0]
    gain_row = norm_gain[0]
    query_heads = query_weight.shape[1] // HEAD_DIM
    key_heads = keyval_weight.shape[1] // (2 * HEAD_DIM)
    last_section = section_id == section_count - 1
    current = held_rows[0]
    whole_rows = lax.all_gather(current, "tp", axis=0, tiled=True)
    caches = []
    leaving = current
    for step_index in range(block_count):
        offset = lax.dynamic_index_in_dim(
            lengths, step_index - section_id + section_count - 1, keepdims=False
        )
        current = lax.dynamic_slice_in_dim(whole_rows, member * shard_count, shard_count, 0)
        block_rows = normalize(whole_rows, gain_row)
        projected = jnp.concatenate(
            [
                jnp.dot(block_rows, query_weight, preferred_element_type=jnp.float32) + query_bias,
                jnp.dot(block_rows, keyval_weight, preferred_element_type=jnp.float32)
                + keyval_bias,
            ],
            axis=1,
        )
        block_cache, attended = attend(
            projected,
            prefix_keys[0, step_index],
            prefix_values[0, step_index],
            offset,
            query_heads,
            key_heads,
            HEAD_DIM,
        )
        caches.append(block_cache)
        summed = lax.psum_scatter(
            jnp.dot(attended, out_weight, preferred_element_type=jnp.float32).astype(jnp.bfloat16),
            "tp",
            scatter_dimension=0,
            tiled=True,
        ).astype(jnp.float32)
        updated = (current.astype(jnp.float32) + summed).astype(jnp.bfloat16)
        if step_index + 1 < block_count:
            payload = jnp.where(last_section, entering[step_index], updated)
            gathered = lax.all_gather(payload, "tp", axis=0, tiled=True)
            whole_rows = from_behind(gathered, "section", 1)
        else:
            leaving = updated
    return (leaving[None], jnp.stack(caches, axis=0)[None])


def solution(mesh):
    return jax.shard_map(
        shards,
        mesh=mesh,
        in_specs=(
            P("section", "tp", None),
            P(None, "tp", None),
            P("section", None),
            P("section", None, "tp"),
            P("section", "tp"),
            P("section", None, "tp"),
            P("section", "tp"),
            P("section", "tp", None),
            P("section", None, None, "tp"),
            P("section", None, None, "tp"),
            P(),
        ),
        out_specs=(P("section", "tp", None), P("section", None, None, "tp")),
        check_vma=False,
    )
```

profile of v0, /device:TPU:8, one launch (start us, length us, event | category | flops | bytes accessed | tf_op | source)
XLA Modules:
  0.0 865.6 jit_solution(9749970957989090668)
XLA Ops:
  10.1 1.9 fusion.189
  12.7 1.5 fusion.194
  14.2 1.3 iota_compare_fusion.1
  15.6 1.3 add_convert_fusion.7
  16.9 1.3 iota_compare_fusion.3
  18.3 1.3 add_convert_fusion.9
  19.6 1.9 slice_bitcast_fusion
  21.5 2.9 multiply_cosine_fusion
  24.5 2.0 fusion.84
  26.5 63.2 %all-gather.12.cloned.1.call-done = bf16[1,256,4096]{2,1,0:T(8,128)(2,1)} async-done(((bf16[1,32,4096]{2,1,0:T(8,128)(2,1)}), bf16[1,256,4096]{2,1,0:T(8,128)(2,1)}) %all-gather.12.cloned.1.call-update) | async-done | bytes 2097168 | tf_op jit(solution)/shard_map/all_gather | solution.py:116
  89.7 2.1 fusion.9
  91.9 2.9 fusion.72
  96.0 1.3 fusion.48
  99.7 1.9 fusion.170
  103.3 1.3 subtract_convert_fusion.3
  104.6 1.8 fusion.28
  109.3 2.7 convolution_convert_fusion.3
  112.1 91.0 %reduce-scatter.5.cloned.1.call-done = bf16[32,4096]{1,0:T(8,128)(2,1)} async-done(((bf16[256,4096]{1,0:T(8,128)(2,1)}), bf16[32,4096]{1,0:T(8,128)(2,1)}) %reduce-scatter.5.cloned.1.call-update) | async-done | bytes 262160 | tf_op jit(solution)/shard_map/reduce_scatter | solution.py:143
  203.1 1.9 fusion.100
  205.1 73.4 %all-gather.6.cloned.1.call-done = bf16[256,4096]{1,0:T(8,128)(2,1)} async-done(((bf16[32,4096]{1,0:T(8,128)(2,1)}), bf16[256,4096]{1,0:T(8,128)(2,1)}) %all-gather.6.cloned.1.call-update) | async-done | bytes 2097168 | tf_op jit(solution)/shard_map/all_gather | solution.py:152
  279.7 27.7 %collective-permute-done = bf16[256,4096]{1,0:T(8,128)(2,1)} collective-permute-done((bf16[256,4096]{1,0:T(8,128)(2,1)}, bf16[256,4096]{1,0:T(8,128)(2,1)}, u32[]{:S(2)}, u32[]{:S(2)}) %collective-permute-start) | collective-permute-done | bytes 2097184 | tf_op jit(solution)/shard_map/ppermute | solution.py:18
  307.4 2.1 fusion
  309.5 2.9 fusion.75
  313.7 2.9 fusion.51
  318.9 1.9 fusion.166
  322.5 1.3 subtract_convert_fusion.2
  323.8 1.8 fusion.29
  328.6 2.6 convolution_convert_fusion.2
  331.3 91.0 %reduce-scatter.7.cloned.1.call-done = bf16[32,4096]{1,0:T(8,128)(2,1)} async-done(((bf16[256,4096]{1,0:T(8,128)(2,1)}), bf16[32,4096]{1,0:T(8,128)(2,1)}) %reduce-scatter.7.cloned.1.call-update) | async-done | bytes 262160 | tf_op jit(solution)/shard_map/reduce_scatter | solution.py:143
  422.3 1.9 fusion.97
  424.3 72.9 %all-gather.8.cloned.1.call-done = bf16[256,4096]{1,0:T(8,128)(2,1)} async-done(((bf16[32,4096]{1,0:T(8,128)(2,1)}), bf16[256,4096]{1,0:T(8,128)(2,1)}) %all-gather.8.cloned.1.call-update) | async-done | bytes 2097168 | tf_op jit(solution)/shard_map/all_gather | solution.py:152
  498.1 27.7 %collective-permute-done.1 = bf16[256,4096]{1,0:T(8,128)(2,1)} collective-permute-done((bf16[256,4096]{1,0:T(8,128)(2,1)}, bf16[256,4096]{1,0:T(8,128)(2,1)}, u32[]{:S(2)}, u32[]{:S(2)}) %collective-permute-start.1) | collective-permute-done | bytes 2097184 | tf_op jit(solution)/shard_map/ppermute | solution.py:18
  525.8 2.1 fusion.3
  527.9 2.9 fusion.78
  532.1 2.9 fusion.54
  541.7 1.7 fusion.30
  546.3 2.7 convolution_convert_fusion.1
  549.0 90.9 %reduce-scatter.9.cloned.1.call-done = bf16[32,4096]{1,0:T(8,128)(2,1)} async-done(((bf16[256,4096]{1,0:T(8,128)(2,1)}), bf16[32,4096]{1,0:T(8,128)(2,1)}) %reduce-scatter.9.cloned.1.call-update) | async-done | bytes 262160 | tf_op jit(solution)/shard_map/reduce_scatter | solution.py:143
  639.9 1.9 fusion.98
  641.9 73.4 %all-gather.10.cloned.1.call-done = bf16[256,4096]{1,0:T(8,128)(2,1)} async-done(((bf16[32,4096]{1,0:T(8,128)(2,1)}), bf16[256,4096]{1,0:T(8,128)(2,1)}) %all-gather.10.cloned.1.call-update) | async-done | bytes 2097168 | tf_op jit(solution)/shard_map/all_gather | solution.py:152
  716.2 27.7 %collective-permute-done.2 = bf16[256,4096]{1,0:T(8,128)(2,1)} collective-permute-done((bf16[256,4096]{1,0:T(8,128)(2,1)}, bf16[256,4096]{1,0:T(8,128)(2,1)}, u32[]{:S(2)}, u32[]{:S(2)}) %collective-permute-start.2) | collective-permute-done | bytes 2097184 | tf_op jit(solution)/shard_map/ppermute | solution.py:18
  743.9 2.1 fusion.6
  746.0 2.9 fusion.81
  750.2 2.9 fusion.57
  758.4 1.7 fusion.31
  763.0 2.7 convolution_convert_fusion
  768.1 88.7 %reduce-scatter.11.cloned.1.call-done = bf16[32,4096]{1,0:T(8,128)(2,1)} async-done(((bf16[256,4096]{1,0:T(8,128)(2,1)}), bf16[32,4096]{1,0:T(8,128)(2,1)}) %reduce-scatter.11.cloned.1.call-update) | async-done | bytes 262160 | tf_op jit(solution)/shard_map/reduce_scatter | solution.py:143
  856.7 1.8 fusion.99
  (187 shorter events, 46.0 us)
Async XLA Ops:
  7.2 84.7 %copy-start = (bf16[1,4096,256]{2,1,0:T(8,128)(2,1)S(1)}, bf16[1,4096,256]{2,1,0:T(8,128)(2,1)}, u32[]{:S(2)}) copy-start(bf16[1,4096,256]{2,1,0:T(8,128)(2,1)} %param.16) | copy-start | bytes 6291460
  7.2 82.5 %all-gather.12.cloned.1.call-start = ((), (), s32[]{:S(2)}) async-start(), calls=%async_computation.11 | async-start | bytes 2359296 | tf_op jit(solution)/shard_map/all_gather | solution.py:116
  7.9 195.2 %reduce-scatter.5.cloned.1.call-start = ((), (), s32[]{:S(2)}) async-start(), calls=%async_computation.4 | async-start | bytes 2359296 | tf_op jit(solution)/shard_map/reduce_scatter | solution.py:143
  9.4 86.6 %copy-start.40 = (f32[1,512]{1,0:T(1,128)}, f32[1,512]{1,0:T(1,128)S(1)}, u32[]{:S(2)}) copy-start(f32[1,512]{1,0:T(1,128)S(1)} %add.267) | copy-start | bytes 6148
  10.1 81.7 %copy-start.44 = (f32[1,256]{1,0:T(1,128)}, f32[1,256]{1,0:T(1,128)S(1)}, u32[]{:S(2)}) copy-start(f32[1,256]{1,0:T(1,128)S(1)} %add.266) | copy-start | bytes 3076
  14.2 10.2 %copy-start.33 = (f32[64]{0:T(128)}, f32[64]{0:T(128)S(1)}, u32[]{:S(2)}) copy-start(f32[64]{0:T(128)S(1)} %multiply_exponential_fusion) | copy-start | bytes 772
  16.9 7.6 copy-start.35
  16.9 7.6 copy-start.37
  19.6 4.9 copy-start.38
  19.6 4.9 copy-start.39
  91.8 4.2 copy-start.5
  91.8 4.2 copy-start.48
  102.5 4.6 copy-start.8
  102.5 3.9 copy-start.7
  112.0 166.9 %copy-start.17 = (bf16[1,1,512,128]{3,2,1,0:T(8,128)(2,1)S(1)}, bf16[1,1,512,128]{3,2,1,0:T(8,128)(2,1)}, u32[]{:S(2)}) copy-start(bf16[1,1,512,128]{3,2,1,0:T(8,128)(2,1)} %get-tuple-element.14) | copy-start | bytes 393220
  112.0 197.4 %copy-start.45 = (f32[1,256]{1,0:T(1,128)S(1)}, f32[1,256]{1,0:T(1,128)}, u32[]{:S(2)}) copy-start(f32[1,256]{1,0:T(1,128)} %copy-done.44) | copy-start | bytes 3076
  112.1 166.4 %all-gather.6.cloned.1.call-start = ((), (), s32[]{:S(2)}) async-start(), calls=%async_computation.5 | async-start | bytes 2359296 | tf_op jit(solution)/shard_map/all_gather | solution.py:152
  205.0 217.3 %reduce-scatter.7.cloned.1.call-start = ((), (), s32[]{:S(2)}) async-start(), calls=%async_computation.6 | async-start | bytes 2359296 | tf_op jit(solution)/shard_map/reduce_scatter | solution.py:143
  278.5 28.9 %collective-permute-start = (bf16[256,4096]{1,0:T(8,128)(2,1)}, bf16[256,4096]{1,0:T(8,128)(2,1)}, u32[]{:S(2)}, u32[]{:S(2)}) collective-permute-start(bf16[256,4096]{1,0:T(8,128)(2,1)} %all-gather.6.cloned.1.call-done), channel_id=1, source_target_pairs={{0,8},{8,16},{16,24},{24,32},{32,40},{40,48},{48,56},{56,64},{64,7... | collective-permute-start | bytes 6291464 | tf_op jit(solution)/shard_map/ppermute | solution.py:18
  309.5 4.2 copy-start.41
  309.5 4.2 copy-start.49
  321.8 4.6 copy-start.10
  321.8 3.9 copy-start.6
  323.8 2.6 copy-start.28
  331.3 166.1 %copy-start.16 = (bf16[1,1,512,128]{3,2,1,0:T(8,128)(2,1)S(1)}, bf16[1,1,512,128]{3,2,1,0:T(8,128)(2,1)}, u32[]{:S(2)}) copy-start(bf16[1,1,512,128]{3,2,1,0:T(8,128)(2,1)} %get-tuple-element.13) | copy-start | bytes 393220
  331.3 196.7 %copy-start.46 = (f32[1,256]{1,0:T(1,128)S(1)}, f32[1,256]{1,0:T(1,128)}, u32[]{:S(2)}) copy-start(f32[1,256]{1,0:T(1,128)} %copy-done.44) | copy-start | bytes 3076
  331.3 165.9 %all-gather.8.cloned.1.call-start = ((), (), s32[]{:S(2)}) async-start(), calls=%async_computation.7 | async-start | bytes 2359296 | tf_op jit(solution)/shard_map/all_gather | solution.py:152
  424.2 215.6 %reduce-scatter.9.cloned.1.call-start = ((), (), s32[]{:S(2)}) async-start(), calls=%async_computation.8 | async-start | bytes 2359296 | tf_op jit(solution)/shard_map/reduce_scatter | solution.py:143
  497.2 28.6 %collective-permute-start.1 = (bf16[256,4096]{1,0:T(8,128)(2,1)}, bf16[256,4096]{1,0:T(8,128)(2,1)}, u32[]{:S(2)}, u32[]{:S(2)}) collective-permute-start(bf16[256,4096]{1,0:T(8,128)(2,1)} %all-gather.8.cloned.1.call-done), channel_id=1, source_target_pairs={{0,8},{8,16},{16,24},{24,32},{32,40},{40,48},{48,56},{56,64},{64,7... | collective-permute-start | bytes 6291464 | tf_op jit(solution)/shard_map/ppermute | solution.py:18
  527.9 4.2 copy-start.42
  527.9 4.2 copy-start.50
  538.6 4.8 copy-start.22
  538.6 4.8 copy-start.24
  539.6 4.5 copy-start.12
  548.9 166.5 %copy-start.15 = (bf16[1,1,512,128]{3,2,1,0:T(8,128)(2,1)S(1)}, bf16[1,1,512,128]{3,2,1,0:T(8,128)(2,1)}, u32[]{:S(2)}) copy-start(bf16[1,1,512,128]{3,2,1,0:T(8,128)(2,1)} %get-tuple-element.12) | copy-start | bytes 393220
  548.9 197.1 %copy-start.47 = (f32[1,256]{1,0:T(1,128)S(1)}, f32[1,256]{1,0:T(1,128)}, u32[]{:S(2)}) copy-start(f32[1,256]{1,0:T(1,128)} %copy-done.44) | copy-start | bytes 3076
  549.0 166.3 %all-gather.10.cloned.1.call-start = ((), (), s32[]{:S(2)}) async-start(), calls=%async_computation.9 | async-start | bytes 2359296 | tf_op jit(solution)/shard_map/all_gather | solution.py:152
  641.8 214.9 %reduce-scatter.11.cloned.1.call-start = ((), (), s32[]{:S(2)}) async-start(), calls=%async_computation.10 | async-start | bytes 2359296 | tf_op jit(solution)/shard_map/reduce_scatter | solution.py:143
  715.2 28.7 %collective-permute-start.2 = (bf16[256,4096]{1,0:T(8,128)(2,1)}, bf16[256,4096]{1,0:T(8,128)(2,1)}, u32[]{:S(2)}, u32[]{:S(2)}) collective-permute-start(bf16[256,4096]{1,0:T(8,128)(2,1)} %all-gather.10.cloned.1.call-done), channel_id=1, source_target_pairs={{0,8},{8,16},{16,24},{24,32},{32,40},{40,48},{48,56},{56,64},{64,7... | collective-permute-start | bytes 6291464 | tf_op jit(solution)/shard_map/ppermute | solution.py:18
  746.0 4.2 copy-start.43
  746.0 4.2 copy-start.51
  753.1 4.0 copy-start.14
  763.0 2.7 copy-start.9
  763.0 2.7 copy-start.18
  763.0 2.7 copy-start.19
  763.0 3.0 copy-start.11
  763.0 3.0 copy-start.20
  763.0 3.0 copy-start.21
  (15 other events, 31.1 us)
Sparse Core Ops, SparseCore 0:
  10.6 79.0 all-gather.11
  112.2 90.8 reduce-scatter.4
  206.7 71.7 all-gather.5
  331.4 90.8 reduce-scatter.6
  425.3 71.8 all-gather.7
  549.1 90.7 reduce-scatter.8
  643.4 71.7 all-gather.9
  765.8 90.8 reduce-scatter.10
where the time goes:
time: 874 us; the launch traced here: 866 us
  waiting for transfers between devices  728 us (83%)
  matrix products  43.4 us (5%)
  other arithmetic  42.2 us (5%)
  local copies, waits for them, and re-layouts  35.4 us (4%)
  between operations  15.3 us (2%)
    reduce_scatter x4, waiting for transfers between devices, shards(): lax.psum_scatter(jnp.dot(attended, out_weight, preferred_element_type=jnp...  361 us
    all_gather x3, waiting for transfers between devices, shards(): gathered = lax.all_gather(payload, 'tp', axis=0, tiled=True)  220 us
    ppermute x3, waiting for transfers between devices, from_behind(): return lax.ppermute(value, axis, pairs)  83 us
    all_gather x1, waiting for transfers between devices, shards(): whole_rows = lax.all_gather(current, 'tp', axis=0, tiled=True)  63.2 us
  transfers between devices with their start and end apart: 11, of which 11 were waited for; matrix products, arithmetic and copies ran while one was open for 3% of the time, Pallas kernels for 0%

commit v1 on v0

v1 whole, which is shorter than its diff:
```python
import functools

import jax
import jax.numpy as jnp
import numpy as np
from jax import lax
from jax.experimental import pallas as pl
from jax.experimental.pallas import tpu as pltpu
from jax.sharding import PartitionSpec as P

MESH = pl.DeviceIdType.MESH
HEAD_DIM = 128
ROPE_BASE = 1000000.0
NORM_EPS = 1e-06
XN = 4
CHUNKS = 4


def relay_kernel(
    dims,
    lengths_ref,
    held_ref,
    entering_ref,
    gain_ref,
    wq_hbm,
    bq_ref,
    wkv_hbm,
    bkv_ref,
    wo_hbm,
    pk_hbm,
    pv_hbm,
    freq_ref,
    cosi_ref,
    sini_ref,
    leaving_ref,
    cache_ref,
    wq,
    wkv,
    wo,
    pk,
    pv,
    xb,
    part,
    rsr,
    zs,
    zr,
    fin,
    load_sem,
    gx_send,
    gx_recv,
    gz_send,
    gz_recv,
    rs_send,
    rs_recv,
    z_send,
    z_recv,
    ag_send,
    ag_recv,
    f_send,
    f_recv,
):
    sections, steps, block, width, shard, prefix, q_heads = dims
    chunk = block // CHUNKS
    piece = chunk // XN
    tiles = steps * CHUNKS
    s = lax.axis_index("section")
    t = lax.axis_index("tp")
    x = lax.rem(t, XN)
    z = t // XN
    nxt = lax.rem(s + 1, sections)
    prv = lax.rem(s + sections - 1, sections)

    def x_peer(d):
        return (s, z * XN + lax.rem(x + d, XN))

    def x_from(d):
        return lax.rem(x + XN - d, XN)

    z_peer = (s, lax.rem(t + XN, 2 * XN))
    z_peer_t = lax.rem(t + XN, 2 * XN)

    loads = [
        pltpu.make_async_copy(src, dst, load_sem.at[n])
        for n, (src, dst) in enumerate(
            [(wq_hbm, wq), (wkv_hbm, wkv), (pk_hbm, pk), (pv_hbm, pv), (wo_hbm, wo)]
        )
    ]
    own = pltpu.make_async_copy(
        held_ref, xb.at[0, pl.ds(pl.multiple_of(t * shard, shard), shard)], load_sem.at[5]
    )
    for copy in loads:
        copy.start()
    own.start()

    barrier = pltpu.get_barrier_semaphore()
    for d in range(1, 2 * XN):
        pl.semaphore_signal(
            barrier, inc=1, device_id=(s, lax.rem(t + d, 2 * XN)), device_id_type=MESH
        )
    for other in (nxt, prv):
        for zz in range(2):
            pl.semaphore_signal(
                barrier, inc=1, device_id=(other, zz * XN + x), device_id_type=MESH
            )
    pl.semaphore_wait(barrier, 2 * XN - 1 + 4)

    def remote(src, dst, send, recv, device):
        return pltpu.make_async_remote_copy(
            src_ref=src,
            dst_ref=dst,
            send_sem=send,
            recv_sem=recv,
            device_id=device,
            device_id_type=MESH,
        )

    def shard_rows(w, member):
        return xb.at[w, pl.ds(pl.multiple_of(member * shard, shard), shard)]

    def gather_x(w, src, plane, member, d):
        return remote(
            src,
            shard_rows(w, member),
            gx_send.at[w, plane, d - 1],
            gx_recv.at[w, plane, d - 1],
            x_peer(d),
        )

    def gather_first(w, src):
        remote(src, shard_rows(w, t), gz_send.at[w], gz_recv.at[w], z_peer).start()
        for d in (1, 3, 2):
            gather_x(w, src, 0, t, d).start()

    def gather_second(w, src):
        remote(src, shard_rows(w, z_peer_t), gz_send.at[w], gz_recv.at[w], z_peer).wait_recv()
        for d in (1, 3, 2):
            gather_x(w, shard_rows(w, z_peer_t), 1, z_peer_t, d).start()

    def gather_arrived(w, c):
        for h in range(2):
            member = 2 * c + h
            xs = lax.rem(member, XN)
            d = lax.rem(x + XN - xs, XN)
            plane = lax.rem(member // XN + z, 2)

            @pl.when(d > 0)
            def _():
                rows = shard_rows(w, member)
                remote(
                    rows,
                    rows,
                    gx_send.at[w, plane, d - 1],
                    gx_recv.at[w, plane, d - 1],
                    (s, t),
                ).wait_recv()

    def gather_sent(w, src):
        remote(src, shard_rows(w, t), gz_send.at[w], gz_recv.at[w], z_peer).wait_send()
        for d in (1, 3, 2):
            gather_x(w, src, 0, t, d).wait_send()
            gather_x(w, shard_rows(w, z_peer_t), 1, z_peer_t, d).wait_send()

    def piece_rows(w, c, owner):
        return xb.at[w, pl.ds(pl.multiple_of(c * chunk + owner * piece, piece), piece)]

    def part_rows(k, owner):
        return part.at[k, pl.ds(pl.multiple_of(owner * piece, piece), piece)]

    def rs_copy(k, d):
        return remote(
            part_rows(k, lax.rem(x + d, XN)),
            rsr.at[k, d - 1],
            rs_send.at[k, d - 1],
            rs_recv.at[k, d - 1],
            x_peer(d),
        )

    def z_copy(k, zz):
        return remote(
            zs.at[k],
            zr.at[k, z],
            z_send.at[k, zz],
            z_recv.at[k, z],
            (nxt, zz * XN + x),
        )

    def ag_copy(k, d):
        rows = piece_rows(k // CHUNKS + 1, lax.rem(k, CHUNKS), x)
        return remote(rows, rows, ag_send.at[k, d - 1], ag_recv.at[k, d - 1], x_peer(d))

    def ag_arrived(k):
        for d in (1, 3, 2):
            rows = piece_rows(k // CHUNKS + 1, lax.rem(k, CHUNKS), x_from(d))
            remote(
                rows, rows, ag_send.at[k, d - 1], ag_recv.at[k, d - 1], x_peer(d)
            ).wait_recv()

    def compute(k):
        w = k // CHUNKS
        c = lax.rem(k, CHUNKS)
        offset = lengths_ref[w - s + sections - 1]
        first = pl.multiple_of(c * chunk, chunk)
        rows = xb[w, pl.ds(first, chunk), :].astype(jnp.float32)
        mean_square = jnp.sum(rows * rows, axis=-1, keepdims=True) * (1.0 / width)
        normed = (
            rows * lax.rsqrt(mean_square + NORM_EPS) * gain_ref[...].astype(jnp.float32)
        ).astype(jnp.bfloat16)
        query = jnp.dot(normed, wq[...], preferred_element_type=jnp.float32)
        query = query + bq_ref[...].astype(jnp.float32)
        keyval = jnp.dot(normed, wkv[...], preferred_element_type=jnp.float32)
        keyval = keyval + bkv_ref[...].astype(jnp.float32)

        base = offset.astype(jnp.float32) * freq_ref[0:1, :]
        cos_b, sin_b = jnp.cos(base), jnp.sin(base)
        cos_i = cosi_ref[pl.ds(first, chunk), :]
        sin_i = sini_ref[pl.ds(first, chunk), :]
        cosine = cos_b * cos_i - sin_b * sin_i
        sine = (sin_b * cos_i + cos_b * sin_i) * freq_ref[1:2, :]

        def turn(v):
            return (v * cosine + pltpu.roll(v, HEAD_DIM // 2, 1) * sine).astype(jnp.bfloat16)

        cache_ref[w, pl.ds(first, chunk), 0:HEAD_DIM] = turn(keyval[:, :HEAD_DIM])
        cache_ref[w, pl.ds(first, chunk), HEAD_DIM:] = keyval[:, HEAD_DIM:].astype(jnp.bfloat16)
        turned = jnp.concatenate(
            [turn(query[:, h * HEAD_DIM : (h + 1) * HEAD_DIM]) for h in range(q_heads)], axis=0
        )

        scale = HEAD_DIM ** (-0.5)
        nt = (((1,), (1,)), ((), ()))
        far = (
            lax.dot_general(turned, pk[w], nt, preferred_element_type=jnp.float32) * scale
        )
        near = (
            lax.dot_general(
                turned, cache_ref[w, :, 0:HEAD_DIM], nt, preferred_element_type=jnp.float32
            )
            * scale
        )
        far_slot = lax.broadcasted_iota(jnp.int32, far.shape, 1)
        near_slot = lax.broadcasted_iota(jnp.int32, near.shape, 1)
        near_row = lax.rem(lax.broadcasted_iota(jnp.int32, near.shape, 0), chunk) + first
        far = jnp.where(far_slot < offset, far, -1e30)
        near = jnp.where(near_slot <= near_row, near, -1e30)
        top = jnp.maximum(
            jnp.max(far, axis=-1, keepdims=True), jnp.max(near, axis=-1, keepdims=True)
        )
        far = jnp.exp(far - top)
        near = jnp.exp(near - top)
        total = jnp.sum(far, axis=-1, keepdims=True) + jnp.sum(near, axis=-1, keepdims=True)
        mixed = jnp.dot(far.astype(jnp.bfloat16), pv[w], preferred_element_type=jnp.float32)
        mixed = mixed + jnp.dot(
            near.astype(jnp.bfloat16),
            cache_ref[w, :, HEAD_DIM:],
            preferred_element_type=jnp.float32,
        )
        mixed = (mixed / total).astype(jnp.bfloat16)
        attended = jnp.concatenate(
            [mixed[h * chunk : (h + 1) * chunk] for h in range(q_heads)], axis=1
        )
        part[k] = jnp.dot(attended, wo[...], preferred_element_type=jnp.float32).astype(
            jnp.bfloat16
        )

    def stage_one(k):
        w = k // CHUNKS
        c = lax.rem(k, CHUNKS)
        gathered = jnp.logical_or(s == 0, w == 0)

        @pl.when(gathered)
        def _():
            gather_arrived(w, c)

        @pl.when(jnp.logical_not(gathered))
        def _():
            ag_arrived(k - CHUNKS)

        compute(k)
        for d in (2, 1, 3):
            rs_copy(k, d).start()

    def stage_two(k):
        w = k // CHUNKS
        c = lax.rem(k, CHUNKS)
        for d in (1, 3, 2):
            rs_copy(k, d).wait_recv()
        rows = pl.ds(pl.multiple_of(c * chunk + x * piece, piece), piece)
        mine = xb[w, rows, :].astype(jnp.float32)
        summed = part[k, pl.ds(pl.multiple_of(x * piece, piece), piece), :].astype(jnp.float32)
        summed = summed + jnp.where(z == 0, mine, 0.0)
        for d in range(XN - 1):
            summed = summed + rsr[k, d].astype(jnp.float32)
        zs[k] = summed.astype(jnp.bfloat16)

        @pl.when(jnp.logical_and(w < steps - 1, s < sections - 1))
        def _():
            for zz in range(2):
                z_copy(k, zz).start()

        @pl.when(w == steps - 1)
        def _():
            owner = 2 * c + x // 2

            @pl.when(owner == t)
            def _():
                fin[z, lax.rem(x, 2)] = zs[k]

            @pl.when(owner != t)
            def _():
                remote(
                    zs.at[k],
                    fin.at[z, lax.rem(x, 2)],
                    f_send.at[c],
                    f_recv.at[z, lax.rem(x, 2)],
                    (s, owner),
                ).start()

        for d in (1, 3, 2):
            rs_copy(k, d).wait_send()

    def stage_three(k):
        for zz in range(2):
            remote(
                zs.at[k],
                zr.at[k, zz],
                z_send.at[k, zz],
                z_recv.at[k, zz],
                (nxt, zz * XN + x),
            ).wait_recv()
        w = k // CHUNKS
        c = lax.rem(k, CHUNKS)
        rows = pl.ds(pl.multiple_of(c * chunk + x * piece, piece), piece)
        xb[w + 1, rows, :] = (zr[k, 0].astype(jnp.float32) + zr[k, 1].astype(jnp.float32)).astype(
            jnp.bfloat16
        )
        for d in (2, 1, 3):
            ag_copy(k, d).start()

    gather_first(0, held_ref)
    cache_ref[...] = jnp.zeros_like(cache_ref)
    gather_second(0, held_ref)
    for copy in loads:
        copy.wait()
    own.wait()

    def body(i, carry):
        @pl.when(i < tiles)
        def _():
            stage_one(i)

        @pl.when(jnp.logical_and(i >= 1, i < tiles + 1))
        def _():
            stage_two(i - 1)

        inner = jnp.logical_and(i >= 2, i < tiles - CHUNKS + 2)

        @pl.when(jnp.logical_and(inner, s > 0))
        def _():
            stage_three(i - 2)

        later = jnp.logical_and(i >= 3, i < tiles - CHUNKS + 3)

        @pl.when(jnp.logical_and(later, s > 0))
        def _():
            for d in (1, 3, 2):
                ag_copy(i - 3, d).wait_send()

        @pl.when(jnp.logical_and(later, s < sections - 1))
        def _():
            for zz in range(2):
                z_copy(i - 3, zz).wait_send()

        entry = jnp.logical_and(s == 0, i < tiles - CHUNKS)
        w_in = i // CHUNKS
        src = entering_ref.at[w_in]

        @pl.when(jnp.logical_and(entry, lax.rem(i, CHUNKS) == 0))
        def _():
            keep = pltpu.make_async_copy(src, shard_rows(w_in + 1, t), load_sem.at[5])
            keep.start()
            gather_first(w_in + 1, src)
            keep.wait()

        @pl.when(jnp.logical_and(entry, lax.rem(i, CHUNKS) == 2))
        def _():
            gather_second(w_in + 1, src)

        @pl.when(jnp.logical_and(entry, lax.rem(i, CHUNKS) == 3))
        def _():
            gather_sent(w_in + 1, src)

        return carry

    lax.fori_loop(0, tiles + 1, body, 0)
    gather_sent(0, held_ref)

    for zz in range(2):
        for h in range(2):
            source = zz * XN + 2 * lax.rem(t, 2) + h

            @pl.when(source != t)
            def _():
                remote(
                    zs.at[0], fin.at[zz, h], f_send.at[0], f_recv.at[zz, h], (s, t)
                ).wait_recv()

    for h in range(2):
        leaving_ref[h * piece : (h + 1) * piece, :] = (
            fin[0, h].astype(jnp.float32) + fin[1, h].astype(jnp.float32)
        ).astype(jnp.bfloat16)
    for c in range(CHUNKS):

        @pl.when(2 * c + x // 2 != t)
        def _():
            remote(
                zs.at[0], fin.at[z, lax.rem(x, 2)], f_send.at[c], f_recv.at[0, 0], (s, t)
            ).wait_send()


def shards(
    held_rows,
    entering,
    norm_gain,
    w_query,
    b_query,
    w_keyval,
    b_keyval,
    w_out,
    prefix_keys,
    prefix_values,
    lengths,
):
    sections = lax.axis_size("section")
    _, shard, width = held_rows.shape
    _, steps, prefix, head_dim = prefix_keys.shape
    members = lax.axis_size("tp")
    block = shard * members
    q_cols = w_query.shape[2]
    kv_cols = w_keyval.shape[2]
    q_heads = q_cols // HEAD_DIM
    tiles = steps * CHUNKS
    piece = block // CHUNKS // XN
    half = HEAD_DIM // 2

    freq = np.exp(-(np.arange(half, dtype=np.float32) * 2.0 / HEAD_DIM) * np.log(ROPE_BASE))
    freq = np.concatenate([freq, freq]).astype(np.float32)
    sign = np.concatenate([-np.ones(half), np.ones(half)]).astype(np.float32)
    angles = np.arange(block, dtype=np.float64)[:, None] * freq[None, :].astype(np.float64)
    freq_sign = np.stack([freq, sign] + [np.zeros_like(freq)] * 6)

    bf16 = jnp.bfloat16
    vmem = pl.BlockSpec(memory_space=pltpu.VMEM)
    hbm = pl.BlockSpec(memory_space=pl.ANY)
    smem = pl.BlockSpec(memory_space=pltpu.SMEM)
    dma = pltpu.SemaphoreType.DMA
    inner = tiles - CHUNKS
    leaving, cache = pl.pallas_call(
        functools.partial(
            relay_kernel, (sections, steps, block, width, shard, prefix, q_heads)
        ),
        out_shape=(
            jax.ShapeDtypeStruct((shard, width), bf16),
            jax.ShapeDtypeStruct((steps, block, kv_cols), bf16),
        ),
        in_specs=[smem, hbm, hbm, vmem, hbm, vmem, hbm, vmem, hbm, hbm, hbm, vmem, vmem, vmem],
        out_specs=(vmem, vmem),
        scratch_shapes=[
            pltpu.VMEM((width, q_cols), bf16),
            pltpu.VMEM((width, kv_cols), bf16),
            pltpu.VMEM((q_cols, width), bf16),
            pltpu.VMEM((steps, prefix, head_dim), bf16),
            pltpu.VMEM((steps, prefix, head_dim), bf16),
            pltpu.VMEM((steps, block, width), bf16),
            pltpu.VMEM((tiles, block // CHUNKS, width), bf16),
            pltpu.VMEM((tiles, XN - 1, piece, width), bf16),
            pltpu.VMEM((tiles, piece, width), bf16),
            pltpu.VMEM((inner, 2, piece, width), bf16),
            pltpu.VMEM((2, 2, piece, width), bf16),
            dma((6,)),
            dma((steps, 2, XN - 1)),
            dma((steps, 2, XN - 1)),
            dma((steps,)),
            dma((steps,)),
            dma((tiles, XN - 1)),
            dma((tiles, XN - 1)),
            dma((inner, 2)),
            dma((inner, 2)),
            dma((inner, XN - 1)),
            dma((inner, XN - 1)),
            dma((CHUNKS,)),
            dma((2, 2)),
        ],
        compiler_params=pltpu.CompilerParams(
            collective_id=0, has_side_effects=True, vmem_limit_bytes=56 * 2**20
        ),
    )(
        lengths,
        held_rows[0],
        entering,
        norm_gain,
        w_query[0],
        b_query,
        w_keyval[0],
        b_keyval,
        w_out[0],
        prefix_keys[0],
        prefix_values[0],
        jnp.asarray(freq_sign, jnp.float32),
        jnp.asarray(np.cos(angles), jnp.float32),
        jnp.asarray(np.sin(angles), jnp.float32),
    )
    return (leaving[None], cache[None])


def solution(mesh):
    return jax.shard_map(
        shards,
        mesh=mesh,
        in_specs=(
            P("section", "tp", None),
            P(None, "tp", None),
            P("section", None),
            P("section", None, "tp"),
            P("section", "tp"),
            P("section", None, "tp"),
            P("section", "tp"),
            P("section", "tp", None),
            P("section", None, None, "tp"),
            P("section", None, None, "tp"),
            P(),
        ),
        out_specs=(P("section", "tp", None), P("section", None, None, "tp")),
        check_vma=False,
    )
```

time: 874 us -> 224 us (0.26)
  the two profiles are of different devices: /device:TPU:8 before, /device:TPU:205 now
where the time goes in v1:
time: 224 us
  Pallas kernels  220 us (98%)
  local copies, waits for them, and re-layouts  3.54 us (2%)
    pallas_call x1, Pallas kernels, shards(): pl.pallas_call(functools.partial(relay_kernel, (sections, steps, block, w...  220 us

profile of v1, /device:TPU:205, one launch (start us, length us, event | category | flops | bytes accessed | tf_op | source)
XLA Modules:
  0.0 224.1 jit_solution(16798232046612491125)
XLA Ops:
  0.6 219.9 %shard_map.149 = (bf16[32,4096]{1,0:T(8,128)(2,1)}, bf16[4,256,256]{2,1,0:T(8,128)(2,1)}) custom-call(s32[35]{0:T(128)} %lengths_ref.1, bf16[32,4096]{1,0:T(8,128)(2,1)} %bitcast.14, bf16[3,32,4096]{2,1,0:T(8,128)(2,1)} %entering_ref.1, bf16[1,4096]{1,0:T(2,128)(2,1)} %gain_ref.1, bf16[4096,512]{1,0:T(8,128)(2,1)} %bitcast.8, bf16[1,512]{1,0:T(2,128)(2,1)} %bq_ref.1, ...), custom_call_target="tpu_custom_call" | custom-call | tf_op jit(solution)/shard_map/pallas_call | solution.py:457
  220.6 1.7 copy.18
  222.2 1.9 copy.19

commit v2 on v1

v2 whole, which is shorter than its diff:
```python
import functools

import jax
import jax.numpy as jnp
import numpy as np
from jax import lax
from jax.experimental import pallas as pl
from jax.experimental.pallas import tpu as pltpu
from jax.sharding import PartitionSpec as P

MESH = pl.DeviceIdType.MESH
HEAD_DIM = 128
ROPE_BASE = 1000000.0
NORM_EPS = 1e-06
XN = 4
CHUNKS = 8
SLOTS = 8
ORDER = (("compute", 0), ("attend", 0), ("relay", 1), ("forward", 6), ("z", 4), ("sum", 2), ("sent", 7))


def relay_kernel(
    dims,
    lengths_ref,
    held_ref,
    entering_ref,
    gain_ref,
    wq_hbm,
    bq_ref,
    wkv_hbm,
    bkv_ref,
    wo_hbm,
    pk_hbm,
    pv_hbm,
    freq_ref,
    cosi_ref,
    sini_ref,
    leaving_ref,
    cache_ref,
    wq,
    wkv,
    wo,
    pk,
    pv,
    xb,
    part,
    relay,
    rsr,
    zs,
    zr,
    fin,
    base,
    turned_ref,
    load_sem,
    gz_send,
    gz_recv,
    g1_send,
    g1_recv,
    g2_send,
    g2_recv,
    rs1_send,
    rs1_recv,
    rs2_send,
    rs2_recv,
    z_send,
    z_recv,
    ag1_send,
    ag1_recv,
    ag2_send,
    ag2_recv,
    f_send,
    f_recv,
):
    sections, steps, block, width, shard, q_heads = dims
    chunk = block // CHUNKS
    half = chunk // 2
    unit = shard // 2
    cols = width // XN
    tiles = steps * CHUNKS
    inner = tiles - CHUNKS
    s = lax.axis_index("section")
    t = lax.axis_index("tp")
    x = lax.rem(t, XN)
    z = t // XN
    nxt = lax.rem(s + 1, sections)
    prv = lax.rem(s + sections - 1, sections)
    at = [lax.rem(x + d, XN) for d in range(XN)]
    step_to = [(s, z * XN + at[1]), (s, z * XN + at[3])]
    came_from = [at[3], at[1]]
    tz = lax.rem(t + XN, 2 * XN)
    z_peer = (s, tz)

    def remote(src, dst, send, recv, device):
        return pltpu.make_async_remote_copy(
            src_ref=src,
            dst_ref=dst,
            send_sem=send,
            recv_sem=recv,
            device_id=device,
            device_id_type=MESH,
        )

    def arrived(ref, recv):
        remote(ref, ref, f_send.at[0], recv, (s, t)).wait_recv()

    def sent(ref, send):
        remote(ref, ref, send, f_recv.at[0, 0], (s, t)).wait_send()

    def ds(start, size):
        return pl.ds(pl.multiple_of(start, size), size)

    loads = [
        pltpu.make_async_copy(src, dst, load_sem.at[n])
        for n, (src, dst) in enumerate(
            [(wq_hbm, wq), (wkv_hbm, wkv), (pk_hbm, pk), (pv_hbm, pv), (wo_hbm, wo)]
        )
    ]

    barrier = pltpu.get_barrier_semaphore()
    for d in range(1, 2 * XN):
        pl.semaphore_signal(
            barrier, inc=1, device_id=(s, lax.rem(t + d, 2 * XN)), device_id_type=MESH
        )
    for other in (nxt, prv):
        for zz in range(2):
            pl.semaphore_signal(
                barrier, inc=1, device_id=(other, zz * XN + x), device_id_type=MESH
            )
    own = pltpu.make_async_copy(held_ref, xb.at[0, ds(t * shard, shard)], load_sem.at[5])
    own.start()
    for copy in loads:
        copy.start()
    pl.semaphore_wait(barrier, 2 * XN - 1 + 4)

    def rows_of(w, member, u):
        return xb.at[w, ds(member * shard + u * unit, unit)]

    def plane_member(plane, position):
        return position + XN * (z if plane == 0 else 1 - z)

    def g_z(w, src, u):
        return remote(
            src.at[pl.ds(u * unit, unit)], rows_of(w, t, u), gz_send.at[w, u], gz_recv.at[w, u], z_peer
        )

    def g_near(w, src, plane, u, way):
        return remote(
            src,
            rows_of(w, plane_member(plane, x), u),
            g1_send.at[w, plane, u, way],
            g1_recv.at[w, plane, u, way],
            step_to[way],
        )

    def g_far(w, plane, u):
        rows = rows_of(w, plane_member(plane, came_from[u]), u)
        return remote(
            rows, rows, g2_send.at[w, plane, u], g2_recv.at[w, plane, u], step_to[u]
        )

    def gather_across(w, src):
        for u in range(2):
            g_z(w, src, u).start()

    def gather_first(w, src):
        for u in range(2):
            for way in range(2):
                g_near(w, src.at[pl.ds(u * unit, unit)], 0, u, way).start()

    def gather_relay(w, plane):
        for u in range(2):
            arrived(
                rows_of(w, plane_member(plane, came_from[u]), u), g1_recv.at[w, plane, u, u]
            )
            g_far(w, plane, u).start()

    def gather_z(w):
        for u in range(2):
            rows = rows_of(w, tz, u)
            arrived(rows, gz_recv.at[w, u])
            for way in range(2):
                g_near(w, rows, 1, u, way).start()

    def gather_chunk(w, c):
        for h in range(chunk // shard):
            member = c * (chunk // shard) + h
            plane = lax.rem(member // XN + z, 2)
            distance = lax.rem(x + XN - lax.rem(member, XN), XN)
            for u in range(2):
                rows = rows_of(w, member, u)

                @pl.when(distance == 1 + 2 * (1 - u))
                def _():
                    arrived(rows, g1_recv.at[w, plane, u, 1 - u])

                @pl.when(distance == 2)
                def _():
                    arrived(rows, g2_recv.at[w, plane, u])

    def gather_sent(w):
        for u in range(2):
            sent(rows_of(w, t, u), gz_send.at[w, u])
            for plane in range(2):
                for way in range(2):
                    sent(rows_of(w, t, u), g1_send.at[w, plane, u, way])
                sent(rows_of(w, t, u), g2_send.at[w, plane, u])

    upper, lower = pl.ds(0, half), pl.ds(half, half)
    halves = [upper, lower]

    def col(owner):
        return ds(owner * cols, cols)

    def slot(k):
        return lax.rem(k, SLOTS)

    def chunk_rows(c, h=None):
        if h is None:
            return ds(c * chunk, chunk)
        return ds(c * chunk + h * half, half)

    def prepare():
        turns = [
            lengths_ref[w - s + sections - 1].astype(jnp.float32) * freq_ref[0:1, :]
            for w in range(steps)
        ]
        base_angles = jnp.concatenate(turns + [turns[0]] * (8 - steps), axis=0)
        base[0] = jnp.cos(base_angles)
        base[1] = jnp.sin(base_angles)

    def project_in(k):
        w = k // CHUNKS
        c = lax.rem(k, CHUNKS)
        here = chunk_rows(c)
        rows = xb[w, here, :].astype(jnp.float32)
        mean_square = jnp.sum(rows * rows, axis=-1, keepdims=True) * (1.0 / width)
        normed = (
            rows * lax.rsqrt(mean_square + NORM_EPS) * gain_ref[...].astype(jnp.float32)
        ).astype(jnp.bfloat16)
        keyval = jnp.dot(normed, wkv[...], preferred_element_type=jnp.float32)
        keyval = keyval + bkv_ref[...].astype(jnp.float32)
        query = jnp.dot(normed, wq[...], preferred_element_type=jnp.float32)
        query = query + bq_ref[...].astype(jnp.float32)

        cos_b = base[0, pl.ds(w, 1), :]
        sin_b = base[1, pl.ds(w, 1), :]
        cos_i = cosi_ref[here, :]
        sin_i = sini_ref[here, :]
        cosine = cos_b * cos_i - sin_b * sin_i
        sine = (sin_b * cos_i + cos_b * sin_i) * freq_ref[1:2, :]

        def turn(v):
            return (v * cosine + pltpu.roll(v, HEAD_DIM // 2, 1) * sine).astype(jnp.bfloat16)

        cache_ref[w, here, 0:HEAD_DIM] = turn(keyval[:, :HEAD_DIM])
        cache_ref[w, here, HEAD_DIM:] = keyval[:, HEAD_DIM:].astype(jnp.bfloat16)
        for h in range(q_heads):
            turned_ref[h * chunk : (h + 1) * chunk, :] = turn(
                query[:, h * HEAD_DIM : (h + 1) * HEAD_DIM]
            )

    def attend(k):
        w = k // CHUNKS
        c = lax.rem(k, CHUNKS)
        offset = lengths_ref[w - s + sections - 1]
        turned = turned_ref[...]
        scale = HEAD_DIM ** (-0.5)
        nt = (((1,), (1,)), ((), ()))
        far = lax.dot_general(turned, pk[w], nt, preferred_element_type=jnp.float32) * scale
        near = (
            lax.dot_general(
                turned, cache_ref[w, :, 0:HEAD_DIM], nt, preferred_element_type=jnp.float32
            )
            * scale
        )
        far_slot = lax.broadcasted_iota(jnp.int32, far.shape, 1)
        near_slot = lax.broadcasted_iota(jnp.int32, near.shape, 1)
        near_row = lax.rem(lax.broadcasted_iota(jnp.int32, near.shape, 0), chunk) + c * chunk
        far = jnp.where(far_slot < offset, far, -1e30)
        near = jnp.where(near_slot <= near_row, near, -1e30)
        top = jnp.maximum(
            jnp.max(far, axis=-1, keepdims=True), jnp.max(near, axis=-1, keepdims=True)
        )
        far = jnp.exp(far - top)
        near = jnp.exp(near - top)
        total = jnp.sum(far, axis=-1, keepdims=True) + jnp.sum(near, axis=-1, keepdims=True)
        mixed = jnp.dot(far.astype(jnp.bfloat16), pv[w], preferred_element_type=jnp.float32)
        mixed = mixed + jnp.dot(
            near.astype(jnp.bfloat16),
            cache_ref[w, :, HEAD_DIM:],
            preferred_element_type=jnp.float32,
        )
        mixed = (mixed / total).astype(jnp.bfloat16)
        return jnp.concatenate(
            [mixed[h * chunk : (h + 1) * chunk] for h in range(q_heads)], axis=1
        )

    def rs_through(k, way):
        return remote(
            part.at[k, halves[way], col(at[2])],
            relay.at[k, way],
            rs1_send.at[slot(k), way, 0],
            rs1_recv.at[k, way, 0],
            step_to[way],
        )

    def rs_near(k, way):
        return remote(
            part.at[k, halves[1 - way], col(came_from[1 - way])],
            rsr.at[k, way, halves[1 - way]],
            rs1_send.at[slot(k), way, 1],
            rs1_recv.at[k, way, 1],
            step_to[way],
        )

    def rs_on(k, way):
        return remote(
            relay.at[k, way],
            rsr.at[k, way, halves[way]],
            rs2_send.at[slot(k), way],
            rs2_recv.at[k, way],
            step_to[way],
        )

    def z_copy(k, zz):
        return remote(
            zs.at[k],
            zr.at[k, z],
            z_send.at[slot(k), zz],
            z_recv.at[k, z],
            (nxt, zz * XN + x),
        )

    def ag_near(k, way):
        rows = xb.at[k // CHUNKS + 1, chunk_rows(lax.rem(k, CHUNKS)), col(x)]
        return remote(
            rows, rows, ag1_send.at[slot(k), way], ag1_recv.at[k, way], step_to[way]
        )

    def ag_far_rows(k, way, owner):
        return xb.at[k // CHUNKS + 1, chunk_rows(lax.rem(k, CHUNKS), way), col(owner)]

    def ag_far(k, way):
        rows = ag_far_rows(k, way, came_from[way])
        return remote(
            rows, rows, ag2_send.at[slot(k), way], ag2_recv.at[k, way], step_to[way]
        )

    def stage_compute(k):
        w = k // CHUNKS
        c = lax.rem(k, CHUNKS)
        gathered = jnp.logical_or(s == 0, w == 0)

        @pl.when(gathered)
        def _():
            gather_chunk(w, c)

        @pl.when(jnp.logical_not(gathered))
        def _():
            for way in range(2):
                arrived(ag_far_rows(k - CHUNKS, way, at[2]), ag2_recv.at[k - CHUNKS, way])

        project_in(k)

    def stage_attend(k):
        attended = attend(k)

        def project(owner):
            part[k, :, col(owner)] = jnp.dot(
                attended, wo[:, col(owner)], preferred_element_type=jnp.float32
            ).astype(jnp.bfloat16)

        project(at[2])
        for way in range(2):
            rs_through(k, way).start()
        project(at[1])
        rs_near(k, 0).start()
        project(at[3])
        rs_near(k, 1).start()
        project(x)

    def stage_relay(k):
        for way in range(2):
            arrived(relay.at[k, way], rs1_recv.at[k, way, 0])
            relay[k, way] = (
                relay[k, way].astype(jnp.float32)
                + part[k, halves[way], col(at[1 if way == 0 else 3])].astype(jnp.float32)
            ).astype(jnp.bfloat16)
            rs_on(k, way).start()

    def stage_sum(k):
        w = k // CHUNKS
        c = lax.rem(k, CHUNKS)
        for way in range(2):
            arrived(rsr.at[k, way, halves[1 - way]], rs1_recv.at[k, way, 1])
            arrived(rsr.at[k, way, halves[way]], rs2_recv.at[k, way])
        mine = xb[w, chunk_rows(c), col(x)].astype(jnp.float32)
        summed = part[k, :, col(x)].astype(jnp.float32) + jnp.where(z == 0, mine, 0.0)
        summed = summed + rsr[k, 0].astype(jnp.float32) + rsr[k, 1].astype(jnp.float32)
        zs[k] = summed.astype(jnp.bfloat16)

        @pl.when(jnp.logical_and(w < steps - 1, s < sections - 1))
        def _():
            for zz in (1 - z, z):
                z_copy(k, zz).start()

        @pl.when(w == steps - 1)
        def _():
            for h in range(chunk // shard):
                owner = c * (chunk // shard) + h
                rows = pl.ds(h * shard, shard)

                @pl.when(owner == t)
                def _():
                    fin[z, :, col(x)] = zs[k, rows, :]

                @pl.when(owner != t)
                def _():
                    remote(
                        zs.at[k, rows],
                        fin.at[z, :, col(x)],
                        f_send.at[owner],
                        f_recv.at[z, x],
                        (s, owner),
                    ).start()

    def stage_z(k):
        for zz in range(2):
            arrived(zr.at[k, zz], z_recv.at[k, zz])
        xb[k // CHUNKS + 1, chunk_rows(lax.rem(k, CHUNKS)), col(x)] = (
            zr[k, 0].astype(jnp.float32) + zr[k, 1].astype(jnp.float32)
        ).astype(jnp.bfloat16)
        for way in range(2):
            ag_near(k, way).start()

    def stage_forward(k):
        w = k // CHUNKS
        rows = chunk_rows(lax.rem(k, CHUNKS))
        for way in range(2):
            arrived(xb.at[w + 1, rows, col(came_from[way])], ag1_recv.at[k, way])
            ag_far(k, way).start()

    def stage_sent(k):
        for way in range(2):
            for n in range(2):
                sent(relay.at[k, way], rs1_send.at[slot(k), way, n])
            sent(relay.at[k, way], rs2_send.at[slot(k), way])

        @pl.when(jnp.logical_and(k < inner, s < sections - 1))
        def _():
            for zz in range(2):
                sent(zs.at[k], z_send.at[slot(k), zz])

        @pl.when(jnp.logical_and(k < inner, s > 0))
        def _():
            for way in range(2):
                sent(zs.at[k], ag1_send.at[slot(k), way])
                sent(relay.at[k, way], ag2_send.at[slot(k), way])

    @pl.when(z == 0)
    def _():
        gather_across(0, held_ref)

    gather_first(0, held_ref)
    cache_ref[...] = jnp.zeros_like(cache_ref)
    prepare()
    gather_relay(0, 0)

    @pl.when(z == 1)
    def _():
        gather_z(0)
        gather_across(0, held_ref)
        gather_relay(0, 1)

    for copy in loads:
        copy.wait()
    own.wait()

    def body(i, carry):
        def staged(after, count, stage, more=True):
            @pl.when(jnp.logical_and(jnp.logical_and(i >= after, i < after + count), more))
            def _():
                stage(i - after)

        calls = dict(
            compute=(tiles, stage_compute, True),
            attend=(tiles, stage_attend, True),
            relay=(tiles, stage_relay, True),
            sum=(tiles, stage_sum, True),
            z=(inner, stage_z, s > 0),
            forward=(inner, stage_forward, s > 0),
            sent=(tiles, stage_sent, True),
        )
        for name, after in ORDER:
            staged(after, *calls[name])

        entry = jnp.logical_and(s == 0, i < inner)
        w_in = i // CHUNKS
        src = entering_ref.at[w_in]

        @pl.when(jnp.logical_and(entry, lax.rem(i, CHUNKS) == 0))
        def _():
            keep = pltpu.make_async_copy(src, xb.at[w_in + 1, ds(t * shard, shard)], load_sem.at[5])
            keep.start()
            gather_across(w_in + 1, src)
            gather_first(w_in + 1, src)
            keep.wait()

        @pl.when(jnp.logical_and(entry, lax.rem(i, CHUNKS) == CHUNKS // 2))
        def _():
            gather_relay(w_in + 1, 0)
            gather_z(w_in + 1)

        @pl.when(jnp.logical_and(entry, lax.rem(i, CHUNKS) == CHUNKS - 2))
        def _():
            gather_relay(w_in + 1, 1)

        @pl.when(jnp.logical_and(z == 0, i == CHUNKS // 4 - 1))
        def _():
            gather_z(0)

        @pl.when(jnp.logical_and(z == 0, i == CHUNKS // 4))
        def _():
            gather_relay(0, 1)

        return carry

    lax.fori_loop(0, tiles + max(after for _, after in ORDER), body, 0)
    gather_sent(0)

    @pl.when(s == 0)
    def _():
        for w in range(1, steps):
            gather_sent(w)

    for zz in range(2):
        for xx in range(XN):

            @pl.when(zz * XN + xx != t)
            def _():
                arrived(fin.at[zz, :, pl.ds(xx * cols, cols)], f_recv.at[zz, xx])

    leaving_ref[...] = (fin[0].astype(jnp.float32) + fin[1].astype(jnp.float32)).astype(
        jnp.bfloat16
    )
    for owner in range(2 * XN):

        @pl.when(owner != t)
        def _():
            sent(fin.at[0, :, pl.ds(0, cols)], f_send.at[owner])


def shards(
    held_rows,
    entering,
    norm_gain,
    w_query,
    b_query,
    w_keyval,
    b_keyval,
    w_out,
    prefix_keys,
    prefix_values,
    lengths,
):
    sections = lax.axis_size("section")
    _, shard, width = held_rows.shape
    _, steps, prefix, head_dim = prefix_keys.shape
    members = lax.axis_size("tp")
    block = shard * members
    q_cols = w_query.shape[2]
    kv_cols = w_keyval.shape[2]
    q_heads = q_cols // HEAD_DIM
    tiles = steps * CHUNKS
    chunk = block // CHUNKS
    cols = width // XN
    half = HEAD_DIM // 2

    freq = np.exp(-(np.arange(half, dtype=np.float32) * 2.0 / HEAD_DIM) * np.log(ROPE_BASE))
    freq = np.concatenate([freq, freq]).astype(np.float32)
    sign = np.concatenate([-np.ones(half), np.ones(half)]).astype(np.float32)
    angles = np.arange(block, dtype=np.float64)[:, None] * freq[None, :].astype(np.float64)
    freq_sign = np.stack([freq, sign] + [np.zeros_like(freq)] * 6)

    bf16 = jnp.bfloat16
    vmem = pl.BlockSpec(memory_space=pltpu.VMEM)
    hbm = pl.BlockSpec(memory_space=pl.ANY)
    smem = pl.BlockSpec(memory_space=pltpu.SMEM)
    dma = pltpu.SemaphoreType.DMA
    inner = tiles - CHUNKS
    leaving, cache = pl.pallas_call(
        functools.partial(
            relay_kernel, (sections, steps, block, width, shard, q_heads)
        ),
        out_shape=(
            jax.ShapeDtypeStruct((shard, width), bf16),
            jax.ShapeDtypeStruct((steps, block, kv_cols), bf16),
        ),
        in_specs=[smem, hbm, hbm, vmem, hbm, vmem, hbm, vmem, hbm, hbm, hbm, vmem, vmem, vmem],
        out_specs=(vmem, vmem),
        scratch_shapes=[
            pltpu.VMEM((width, q_cols), bf16),
            pltpu.VMEM((width, kv_cols), bf16),
            pltpu.VMEM((q_cols, width), bf16),
            pltpu.VMEM((steps, prefix, head_dim), bf16),
            pltpu.VMEM((steps, prefix, head_dim), bf16),
            pltpu.VMEM((steps, block, width), bf16),
            pltpu.VMEM((tiles, chunk, width), bf16),
            pltpu.VMEM((tiles, 2, chunk // 2, cols), bf16),
            pltpu.VMEM((tiles, 2, chunk, cols), bf16),
            pltpu.VMEM((tiles, chunk, cols), bf16),
            pltpu.VMEM((inner, 2, chunk, cols), bf16),
            pltpu.VMEM((2, shard, width), bf16),
            pltpu.VMEM((2, 8, HEAD_DIM), jnp.float32),
            pltpu.VMEM((q_cols // HEAD_DIM * chunk, HEAD_DIM), bf16),
            dma((6,)),
            dma((steps, 2)),
            dma((steps, 2)),
            dma((steps, 2, 2, 2)),
            dma((steps, 2, 2, 2)),
            dma((steps, 2, 2)),
            dma((steps, 2, 2)),
            dma((SLOTS, 2, 2)),
            dma((tiles, 2, 2)),
            dma((SLOTS, 2)),
            dma((tiles, 2)),
            dma((SLOTS, 2)),
            dma((inner, 2)),
            dma((SLOTS, 2)),
            dma((inner, 2)),
            dma((SLOTS, 2)),
            dma((inner, 2)),
            dma((members,)),
            dma((2, XN)),
        ],
        compiler_params=pltpu.CompilerParams(
            collective_id=0, has_side_effects=True, vmem_limit_bytes=56 * 2**20
        ),
    )(
        lengths,
        held_rows[0],
        entering,
        norm_gain,
        w_query[0],
        b_query,
        w_keyval[0],
        b_keyval,
        w_out[0],
        prefix_keys[0],
        prefix_values[0],
        jnp.asarray(freq_sign, jnp.float32),
        jnp.asarray(np.cos(angles), jnp.float32),
        jnp.asarray(np.sin(angles), jnp.float32),
    )
    return (leaving[None], cache[None])


def solution(mesh):
    return jax.shard_map(
        shards,
        mesh=mesh,
        in_specs=(
            P("section", "tp", None),
            P(None, "tp", None),
            P("section", None),
            P("section", None, "tp"),
            P("section", "tp"),
            P("section", None, "tp"),
            P("section", "tp"),
            P("section", "tp", None),
            P("section", None, None, "tp"),
            P("section", None, None, "tp"),
            P(),
        ),
        out_specs=(P("section", "tp", None), P("section", None, None, "tp")),
        check_vma=False,
    )
```

time: 224 us -> 202 us (0.902)
  the two profiles are of different devices: /device:TPU:205 before, /device:TPU:2 now
where the time goes in v2:
time: 202 us
  Pallas kernels  198 us (98%)
  local copies, waits for them, and re-layouts  3.54 us (2%)
    pallas_call x1, Pallas kernels, shards(): pl.pallas_call(functools.partial(relay_kernel, (sections, steps, block, w...  198 us

profile of v2, /device:TPU:2, one launch (start us, length us, event | category | flops | bytes accessed | tf_op | source)
XLA Modules:
  0.0 202.1 jit_solution(2659624987716454956)
XLA Ops:
  0.6 197.9 %shard_map.149 = (bf16[32,4096]{1,0:T(8,128)(2,1)}, bf16[4,256,256]{2,1,0:T(8,128)(2,1)}) custom-call(s32[35]{0:T(128)} %lengths_ref.1, bf16[32,4096]{1,0:T(8,128)(2,1)} %bitcast.14, bf16[3,32,4096]{2,1,0:T(8,128)(2,1)} %entering_ref.1, bf16[1,4096]{1,0:T(2,128)(2,1)} %gain_ref.1, bf16[4096,512]{1,0:T(8,128)(2,1)} %bitcast.8, bf16[1,512]{1,0:T(2,128)(2,1)} %bq_ref.1, ...), custom_call_target="tpu_custom_call" | custom-call | tf_op jit(solution)/shard_map/pallas_call | solution.py:590
  198.5 1.7 copy.18
  200.2 1.9 copy.19

commit v3 on v2

--- a/solution.py
+++ b/solution.py
@@ -15,7 +15,7 @@
 XN = 4
 CHUNKS = 8
 SLOTS = 8
-ORDER = (("compute", 0), ("attend", 0), ("relay", 1), ("forward", 6), ("z", 4), ("sum", 2), ("sent", 7))
+ORDER = (("relay", 2), ("compute", 0), ("z", 5), ("attend", 0), ("sum", 3), ("forward", 6), ("sent", 7))
 
 
 def relay_kernel(
@@ -73,7 +73,6 @@
     sections, steps, block, width, shard, q_heads = dims
     chunk = block // CHUNKS
     half = chunk // 2
-    unit = shard // 2
     cols = width // XN
     tiles = steps * CHUNKS
     inner = tiles - CHUNKS
@@ -132,14 +131,18 @@
     pl.semaphore_wait(barrier, 2 * XN - 1 + 4)
 
     def rows_of(w, member, u):
-        return xb.at[w, ds(member * shard + u * unit, unit)]
+        return xb.at[w, ds(member * shard, shard), pl.ds(u * cols, cols)]
 
     def plane_member(plane, position):
         return position + XN * (z if plane == 0 else 1 - z)
 
     def g_z(w, src, u):
         return remote(
-            src.at[pl.ds(u * unit, unit)], rows_of(w, t, u), gz_send.at[w, u], gz_recv.at[w, u], z_peer
+            src.at[:, pl.ds(u * cols, cols)],
+            rows_of(w, t, u),
+            gz_send.at[w, u],
+            gz_recv.at[w, u],
+            z_peer,
         )
 
     def g_near(w, src, plane, u, way):
@@ -152,52 +155,61 @@
         )
 
     def g_far(w, plane, u):
-        rows = rows_of(w, plane_member(plane, came_from[u]), u)
-        return remote(
-            rows, rows, g2_send.at[w, plane, u], g2_recv.at[w, plane, u], step_to[u]
+        way = u % 2
+        rows = rows_of(w, plane_member(plane, came_from[way]), u)
+        return remote(
+            rows, rows, g2_send.at[w, plane, u], g2_recv.at[w, plane, u], step_to[way]
         )
 
     def gather_across(w, src):
-        for u in range(2):
+        for u in range(XN):
             g_z(w, src, u).start()
 
     def gather_first(w, src):
-        for u in range(2):
+        for u in range(XN):
             for way in range(2):
-                g_near(w, src.at[pl.ds(u * unit, unit)], 0, u, way).start()
+                g_near(w, src.at[:, pl.ds(u * cols, cols)], 0, u, way).start()
+
+    def relay_unit(w, plane, u):
+        way = u % 2
+        arrived(
+            rows_of(w, plane_member(plane, came_from[way]), u), g1_recv.at[w, plane, u, way]
+        )
+        g_far(w, plane, u).start()
 
     def gather_relay(w, plane):
-        for u in range(2):
-            arrived(
-                rows_of(w, plane_member(plane, came_from[u]), u), g1_recv.at[w, plane, u, u]
-            )
-            g_far(w, plane, u).start()
+        for u in range(XN):
+            relay_unit(w, plane, u)
+
+    def z_unit(w, u):
+        rows = rows_of(w, tz, u)
+        arrived(rows, gz_recv.at[w, u])
+        for way in range(2):
+            g_near(w, rows, 1, u, way).start()
 
     def gather_z(w):
-        for u in range(2):
-            rows = rows_of(w, tz, u)
-            arrived(rows, gz_recv.at[w, u])
-            for way in range(2):
-                g_near(w, rows, 1, u, way).start()
+        for u in range(XN):
+            z_unit(w, u)
 
     def gather_chunk(w, c):
         for h in range(chunk // shard):
             member = c * (chunk // shard) + h
             plane = lax.rem(member // XN + z, 2)
             distance = lax.rem(x + XN - lax.rem(member, XN), XN)
-            for u in range(2):
+            for u in range(XN):
                 rows = rows_of(w, member, u)
-
-                @pl.when(distance == 1 + 2 * (1 - u))
+                other = 1 - u % 2
+
+                @pl.when(distance == 1 + 2 * other)
                 def _():
-                    arrived(rows, g1_recv.at[w, plane, u, 1 - u])
+                    arrived(rows, g1_recv.at[w, plane, u, other])
 
                 @pl.when(distance == 2)
                 def _():
                     arrived(rows, g2_recv.at[w, plane, u])
 
     def gather_sent(w):
-        for u in range(2):
+        for u in range(XN):
             sent(rows_of(w, t, u), gz_send.at[w, u])
             for plane in range(2):
                 for way in range(2):
@@ -463,11 +475,16 @@
     gather_first(0, held_ref)
     cache_ref[...] = jnp.zeros_like(cache_ref)
     prepare()
-    gather_relay(0, 0)
+
+    @pl.when(z == 0)
+    def _():
+        gather_relay(0, 0)
 
     @pl.when(z == 1)
     def _():
-        gather_z(0)
+        for u in range(XN):
+            relay_unit(0, 0, u)
+            z_unit(0, u)
         gather_across(0, held_ref)
         gather_relay(0, 1)
 
@@ -613,12 +630,12 @@
             pltpu.VMEM((2, 8, HEAD_DIM), jnp.float32),
             pltpu.VMEM((q_cols // HEAD_DIM * chunk, HEAD_DIM), bf16),
             dma((6,)),
-            dma((steps, 2)),
-            dma((steps, 2)),
-            dma((steps, 2, 2, 2)),
-            dma((steps, 2, 2, 2)),
-            dma((steps, 2, 2)),
-            dma((steps, 2, 2)),
+            dma((steps, XN)),
+            dma((steps, XN)),
+            dma((steps, 2, XN, 2)),
+            dma((steps, 2, XN, 2)),
+            dma((steps, 2, XN)),
+            dma((steps, 2, XN)),
             dma((SLOTS, 2, 2)),
             dma((tiles, 2, 2)),
             dma((SLOTS, 2)),

time: 202 us -> 193 us (0.955)
  the two profiles are of different devices: /device:TPU:2 before, /device:TPU:8 now
where the time goes in v3:
time: 193 us; the launch traced here: 190 us
  Pallas kernels  185 us (96%)
  local copies, waits for them, and re-layouts  3.54 us (2%)
    pallas_call x1, Pallas kernels, shards(): pl.pallas_call(functools.partial(relay_kernel, (sections, steps, block, w...  185 us

profile of v3, /device:TPU:8, one launch (start us, length us, event | category | flops | bytes accessed | tf_op | source)
XLA Modules:
  0.0 189.7 jit_solution(14489403352059912409)
XLA Ops:
  0.6 185.5 %shard_map.149 = (bf16[32,4096]{1,0:T(8,128)(2,1)}, bf16[4,256,256]{2,1,0:T(8,128)(2,1)}) custom-call(s32[35]{0:T(128)} %lengths_ref.1, bf16[32,4096]{1,0:T(8,128)(2,1)} %bitcast.14, bf16[3,32,4096]{2,1,0:T(8,128)(2,1)} %entering_ref.1, bf16[1,4096]{1,0:T(2,128)(2,1)} %gain_ref.1, bf16[4096,512]{1,0:T(8,128)(2,1)} %bitcast.8, bf16[1,512]{1,0:T(2,128)(2,1)} %bq_ref.1, ...), custom_call_target="tpu_custom_call" | custom-call | tf_op jit(solution)/shard_map/pallas_call | solution.py:607
  186.1 1.7 copy.18
  187.8 1.9 copy.19
